TPU v7x, 32 devices: a whole 2x2x4 slice. The times are simulated.
32 devices in a mesh: win: 2 (over y), lon: 8 (over z, x), lat: 2 (over core).
Axes of the slice: x: 2, y: 2, z: 4, core: 2. Of those that a mesh axis runs over, the one named last changes fastest.
Arguments:
- dual_state: float32 [2, 16, 2, 4096], P('win', None, 'lat', 'lon'), may hold values from -6 to 6
- dual_obs: float32 [2, 16, 2, 4096], P('win', None, 'lat', 'lon'), may hold values from -6 to 6
- increment: float32 [2, 16, 2, 4096], P('win', None, 'lat', 'lon'), may hold values from -6 to 6
- resid_dual: float32 [2, 16, 2, 4096], P('win', None, 'lat', 'lon'), may hold values from -6 to 6
- resid_obs: float32 [2, 16, 2, 4096], P('win', None, 'lat', 'lon'), may hold values from -6 to 6
- resid_incr: float32 [2, 16, 2, 4096], P('win', None, 'lat', 'lon'), may hold values from -6 to 6
- search_dual: float32 [2, 16, 2, 4096], P('win', None, 'lat', 'lon'), may hold values from -6 to 6
- search_obs: float32 [2, 16, 2, 4096], P('win', None, 'lat', 'lon'), may hold values from -6 to 6
- search_incr: float32 [2, 16, 2, 4096], P('win', None, 'lat', 'lon'), may hold values from -6 to 6
- ensemble: bfloat16 [2, 64, 16, 2, 4096], P('win', None, None, 'lat', 'lon'), may hold values from -12 to 12
- tangent_coefs: float32 [2, 5, 16, 2, 4096], P('win', None, None, 'lat', 'lon'), may hold values from -0.25 to 0.25
- obs_weight: float32 [2, 16, 2, 4096], P('win', None, 'lat', 'lon'), may hold values from 0.25 to 2
- obs_var: float32 [2, 16, 2, 4096], P('win', None, 'lat', 'lon'), may hold values from 0.5 to 2
- loc_cols: int32 [8, 5], P('lon'), may hold values from 0 to 7, as said below
- loc_vals: bfloat16 [8, 5, 512, 512], P('lon'), may hold values from -0.125 to 0.125
Outputs:
- next_dual: float32 [2, 16, 2, 4096], P('win', None, 'lat', 'lon')
- next_obs: float32 [2, 16, 2, 4096], P('win', None, 'lat', 'lon')
- next_incr: float32 [2, 16, 2, 4096], P('win', None, 'lat', 'lon')
- next_res_dual: float32 [2, 16, 2, 4096], P('win', None, 'lat', 'lon')
- next_res_obs: float32 [2, 16, 2, 4096], P('win', None, 'lat', 'lon')
- next_res_incr: float32 [2, 16, 2, 4096], P('win', None, 'lat', 'lon')
Inputs may be any that keep to these rules, and one draw needn't show every extreme that they name: `loc_cols`: row block i names 5 distinct column blocks, block i itself among them, each within 3 blocks of i around the longitude loop.
All inputs are finite; a program needn't handle non-finite values.
Results may differ from a plain program's by a relative error of at most 0.0017.
Values may be sent and summed in bfloat16 or wider, within the bound.
A program may use at most 64 MiB of HBM per device.

v0:
```python
import functools

import jax
import jax.numpy as jnp
from jax import lax
from jax.experimental import pallas as pl
from jax.experimental.pallas import tpu as pltpu
from jax.sharding import PartitionSpec as P

CHUNKS = 8
EARLY = 2
WEIGHTS = 4
LAG = 4
LANES = 128
MESH = pl.DeviceIdType.MESH
BF16 = jnp.bfloat16
F32 = jnp.float32


def remote(src, dst, send, recv, where):
    return pltpu.make_async_remote_copy(
        src_ref=src,
        dst_ref=dst,
        send_sem=send,
        recv_sem=recv,
        device_id=where,
        device_id_type=MESH,
    )


def kernel(
    sizes,
    dual_state_h, dual_obs_h, increment_h,
    resid_dual_h, resid_obs_h, resid_incr_h,
    search_dual_h, search_obs_h, search_incr_h,
    ens_h, coefs_h, obs_weight_h, obs_var_h, cols, vals_h,
    out,
    dual_state, dual_obs, increment,
    resid_dual, resid_obs, resid_incr,
    search_dual, search_obs, search_incr,
    ens, coefs, obs_weight, obs_var, vals, load,
    near, hold, near_s, own_s, w_home, w_out, w_in,
    g_own, g_lat, g_edge, g_side,
    part, part_lon, pair, part_col,
    moved, moved_in, acc, back, covar_flat,
    e_send, e_recv, s_send, s_recv, w_send, w_recv, f_send, f_recv, h_send, h_recv,
    g_send, g_recv, a_send, a_recv, b_send, b_recv,
    m_send, m_recv, r_send, r_recv,
):
    wins, bands, lats, members, levels, block = sizes
    colors = wins * lats
    pieces = block // LANES
    flat = levels * pieces
    rows = members * levels // CHUNKS
    group = rows // levels
    share = block // colors
    win = lax.axis_index("win")
    lon = lax.axis_index("lon")
    lat = lax.axis_index("lat")
    color = win * lats + lat

    def at(lon_step=0, other_lat=False, win_step=0):
        return {
            "win": lax.rem(win + win_step + wins, wins),
            "lon": lax.rem(lon + lon_step + bands, bands),
            "lat": 1 - lat if other_lat else lat,
        }

    def peer(step):
        index = lax.rem(color + step, colors)
        return index, {"win": index // lats, "lon": lon, "lat": lax.rem(index, lats)}

    barrier = pltpu.get_barrier_semaphore()
    greeted = [at(step) for step in range(1, bands)]
    greeted += [peer(step)[1] for step in range(1, colors)]
    greeted += [at(1, True), at(-1, True)]
    for where in greeted:
        pl.semaphore_signal(barrier, inc=1, device_id=where, device_id_type=MESH)

    loads = [
        pltpu.make_async_copy(source, target, load.at[k])
        for k, (source, target) in enumerate((
            (ens_h, ens), (search_dual_h, search_dual), (search_incr_h, search_incr),
            (vals_h, vals), (coefs_h, coefs), (search_obs_h, search_obs),
            (resid_dual_h, resid_dual), (resid_obs_h, resid_obs), (resid_incr_h, resid_incr),
            (dual_state_h, dual_state), (dual_obs_h, dual_obs), (increment_h, increment),
            (obs_weight_h, obs_weight), (obs_var_h, obs_var),
        ))
    ]
    for copy in loads:
        copy.start()

    started = []

    def go(copy):
        copy.start()
        started.append(copy)

    parity = lax.rem(lon, 2)
    even = parity == 0

    def lines(t):
        return pl.ds(pl.multiple_of(t * rows, rows), rows)

    def to_west(t):
        return remote(ens.at[lines(t)], near.at[1, lines(t)], e_send.at[0, t], e_recv.at[0, t], at(-2))

    def to_east(t):
        return remote(ens.at[lines(t)], near.at[0, lines(t)], e_send.at[1, t], e_recv.at[1, t], at(1))

    def by_relay(t):
        return jnp.logical_or(t < 3, lax.rem(t, 2) == 0)

    def to_relay(t):
        way = -1
        return remote(ens.at[lines(t)], hold.at[lines(t)], e_send.at[1, t], e_recv.at[2, t], at(way))

    def from_relay(t):
        return remote(hold.at[lines(t)], near.at[0, lines(t)], e_send.at[2, t], e_recv.at[1, t], at(2))

    def first_sends(t, carry):
        direct_first = lat == 0

        @pl.when(direct_first)
        def _():
            to_west(t).start()

        relay = jnp.logical_and(jnp.logical_not(even), by_relay(t))

        @pl.when(jnp.logical_not(relay))
        def _():
            to_east(t).start()

        @pl.when(relay)
        def _():
            to_relay(t).start()

        @pl.when(jnp.logical_not(direct_first))
        def _():
            to_west(t).start()

        return carry

    def relayed(t, carry):
        @pl.when(jnp.logical_and(parity == 0, by_relay(t)))
        def _():
            to_relay(t).wait_recv()
            from_relay(t).start()

        return carry

    loads[0].wait()
    pl.semaphore_wait(barrier, len(greeted))
    lax.fori_loop(0, 1, first_sends, 0)

    def slot_of(step):
        target = lax.rem(lon + step + bands, bands)
        slot = jnp.int32(0)
        found = jnp.int32(0)
        for j in range(vals.shape[0]):
            hit = cols[0, j] == target
            slot = jnp.where(hit, j, slot)
            found = jnp.where(hit, 1, found)
        return slot, found > 0

    mine = pl.ds(pl.multiple_of(color * share, share), share)
    loads[3].wait()
    for k, step in enumerate((1, 3, -2, -3)):
        slot, found = slot_of(step)
        w_out[k] = jnp.where(found, vals[slot, mine, :], jnp.zeros((share, block), BF16))

    def rows_of(ref, base):
        return [ref[pl.ds(base + j, levels, stride=pieces), :] for j in range(pieces)]

    loads[1].wait()
    loads[2].wait()
    for j, (u, v) in enumerate(zip(rows_of(search_dual, 0), rows_of(search_incr, 0))):
        own_s[:, pl.ds(j * LANES, LANES)] = u
        g_own[0, :, pl.ds(j * LANES, LANES)] = v
        g_own[1, :, pl.ds(j * LANES, LANES)] = u

    ways = (1, -2)
    for k, way in enumerate(ways):
        go(remote(own_s, near_s.at[k], s_send.at[k], s_recv.at[k], at(way)))
        both = pl.ds(2 * k, 2)
        go(remote(w_out.at[both], w_in.at[both, mine], w_send.at[k], w_recv.at[k], at(way)))

    lax.fori_loop(1, 2 * EARLY, first_sends, 0)

    loads[4].wait()
    for c in range(5):
        for j, value in enumerate(rows_of(coefs, c * flat)):
            g_own[2 + c, :, pl.ds(j * LANES, LANES)] = value
    lane = lax.broadcasted_iota(jnp.int32, (levels, LANES), 1)
    lead = g_own[0, :, pl.ds(0, LANES)]
    last = pltpu.roll(g_own[0, :, pl.ds(block - LANES, LANES)], 2, 1)
    for k in range(1, 7):
        chosen = lane // 2 == k
        lead = jnp.where(chosen, pltpu.roll(g_own[k, :, pl.ds(0, LANES)], 2 * k, 1), lead)
        last = jnp.where(chosen, pltpu.roll(g_own[k, :, pl.ds(block - LANES, LANES)], 2 * k + 2, 1), last)
    g_edge[0] = last
    g_edge[1] = lead

    go(remote(g_own, g_lat, g_send.at[0], g_recv.at[0], at(0, True)))

    def edge(side, other):
        n = 1 + 2 * side + other
        way = 1 - 2 * side
        return remote(g_edge.at[side], g_side.at[side, other], g_send.at[n], g_recv.at[n], at(way, other == 1))

    for side in range(2):
        for other in range(2):
            go(edge(side, other))

    for copy in loads[5:]:
        copy.wait()
    resid_sq = jnp.sum(resid_dual[...] ** 2 + resid_obs[...] ** 2 + resid_incr[...] ** 2)
    search_sq = jnp.sum(search_dual[...] ** 2 + search_obs[...] ** 2 + search_incr[...] ** 2)
    first_row = lax.broadcasted_iota(jnp.int32, (8, LANES), 0) == 0
    part[...] = jnp.where(first_row, resid_sq, search_sq)
    part_lon[lon] = part[...]
    for step in range(1, bands):
        go(remote(part, part_lon.at[lon], a_send.at[step], a_recv.at[lon], at(step)))

    for d, step in enumerate((0, -1, 2)):
        slot, found = slot_of(step)
        w_home[d] = jnp.where(found, vals[slot], jnp.zeros((block, block), BF16))
    acc[...] = jnp.zeros_like(acc)

    every = pl.ds(0, WEIGHTS)
    for k in range(2):
        both = pl.ds(2 * k, 2)
        remote(w_out.at[both], w_in.at[both, mine], w_send.at[k], w_recv.at[k], at(0)).wait_recv()
    spot = w_in.at[every, mine]
    for step in range(1, wins):
        go(remote(spot, spot, f_send.at[step], f_recv.at[win], at(0, False, step)))
    lax.fori_loop(0, EARLY, relayed, 0)
    lax.fori_loop(2 * EARLY, 3 * EARLY, first_sends, 0)

    remote(g_own, g_lat, g_send.at[0], g_recv.at[0], at(0)).wait_recv()
    for side in range(2):
        for other in range(2):
            edge(side, other).wait_recv()

    def wide(k, other):
        middle = g_lat if other else g_own
        before = pltpu.roll(g_side[0, other], LANES - 2 - 2 * k, 1)
        after = pltpu.roll(g_side[1, other], (LANES - 2 * k) % LANES, 1)
        return jnp.concatenate([before, middle[k], after], axis=1)

    span = block + 2 * LANES

    def east(x):
        return pltpu.roll(x, span - 1, 1)

    def west(x):
        return pltpu.roll(x, 1, 1)

    here = [wide(k, 0) for k in range(7)]
    over = [wide(k, 1) for k in range(7)]
    south_row = lat == 0
    cross = jnp.where(south_row, here[5], here[6])
    cross_over = jnp.where(south_row, over[6], over[5])

    def forward(v, beyond, c, between):
        return (0.5 + c[2]) * v + c[3] * east(v) + c[4] * west(v) + between * beyond

    def adjoint(u, beyond, c, between):
        return (0.5 + c[2]) * u + west(c[3] * u) + east(c[4] * u) + between * beyond

    once = forward(here[0], over[0], here, cross)
    once_over = forward(over[0], here[0], over, cross_over)
    twice = forward(once, once_over, here, cross)
    back_once = adjoint(here[1], over[1], here, cross_over)
    back_over = adjoint(over[1], here[1], over, cross)
    back_twice = adjoint(back_once, back_over, here, cross_over)
    for j in range(pieces):
        cut = slice((j + 1) * LANES, (j + 2) * LANES)
        moved[0, pl.ds(j, levels, stride=pieces), :] = twice[:, cut]
        moved[1, pl.ds(j, levels, stride=pieces), :] = back_twice[:, cut]
    for k, way in enumerate((1, -1)):
        go(remote(moved.at[k], moved_in.at[k], m_send.at[k], m_recv.at[k], at(0, False, way)))

    for step in range(1, bands):
        source = lax.rem(lon + step, bands)
        remote(part, part_lon.at[source], a_send.at[step], a_recv.at[source], at(0)).wait_recv()
    pair[...] = jnp.sum(part_lon[...], axis=0)
    part_col[color] = pair[...]
    for step in range(1, colors):
        _, where = peer(step)
        go(remote(pair, part_col.at[color], b_send.at[step], b_recv.at[color], where))

    for step in range(1, wins):
        source = lax.rem(win + step, wins)
        remote(spot, spot, f_send.at[step], f_recv.at[source], at(0)).wait_recv()

    def over_lat(w, holder):
        theirs = pl.ds(pl.multiple_of((w * lats + holder) * share, share), share)
        place = w_in.at[every, theirs]
        return remote(place, place, h_send.at[w], h_recv.at[w], at(0, True))

    for w in range(wins):
        go(over_lat(w, lat))
    lax.fori_loop(3 * EARLY, CHUNKS, first_sends, 0)
    for k in range(2):
        remote(own_s, near_s.at[k], s_send.at[k], s_recv.at[k], at(0)).wait_recv()

    def spread_of(t):
        def read(ref, search):
            member = ref[...].astype(F32).reshape(group, levels, block)
            product = (member * search[None]).astype(BF16).reshape(rows, block)
            return member, product

        def weigh(member, terms):
            total = sum(jnp.dot(p, w, preferred_element_type=F32) for p, w in terms)
            return jnp.sum(member * total.reshape(group, levels, block), axis=0)

        member, product = read(ens.at[lines(t)], own_s[...])
        first, first_product = read(near.at[0, lines(t)], near_s[0])
        second, second_product = read(near.at[1, lines(t)], near_s[1])
        acc[0] += weigh(member, ((product, w_home[0]), (first_product, w_home[1]), (second_product, w_home[2])))
        acc[1] += weigh(first, ((product, w_in[0]), (second_product, w_in[1])))
        acc[2] += weigh(second, ((product, w_in[2]), (first_product, w_in[3])))

    def step_of(t, carry):
        @pl.when(jnp.logical_and(t >= EARLY, t < CHUNKS))
        def _():
            relayed(t, 0)

        @pl.when(t == LAG)
        def _():
            for w in range(wins):
                over_lat(w, 1 - lat).wait_recv()

        @pl.when(t >= LAG)
        def _():
            to_west(t - LAG).wait_recv()
            to_east(t - LAG).wait_recv()
            spread_of(t - LAG)

        return carry

    lax.fori_loop(0, CHUNKS + LAG, step_of, 0)

    for k, way in enumerate(ways):
        go(remote(acc.at[1 + k], back.at[k], r_send.at[k], r_recv.at[k], at(-way)))

    for step in range(1, colors):
        source, where = peer(step)
        remote(pair, part_col.at[source], b_send.at[step], b_recv.at[source], where).wait_recv()
    sums = jnp.sum(part_col[...], axis=0)
    alpha = sums[0:1, :] / (sums[1:2, :] + 1e-6)

    out[0] = dual_state[...] + alpha * search_dual[...]
    out[1] = dual_obs[...] + alpha * search_obs[...]
    out[2] = increment[...] + alpha * search_incr[...]
    image_obs = obs_var[...] * search_obs[...] + obs_weight[...] * search_incr[...]
    out[4] = resid_obs[...] - alpha * image_obs
    for k in range(2):
        remote(moved.at[k], moved_in.at[k], m_send.at[k], m_recv.at[k], at(0)).wait_recv()
    later = jnp.where(win < wins - 1, moved_in[1], 0.0)
    image_incr = search_dual[...] - later + obs_weight[...] * search_obs[...]
    out[5] = resid_incr[...] - alpha * image_incr
    prior = jnp.where(win > 0, moved_in[0], 0.0)

    for k in range(2):
        remote(acc.at[1 + k], back.at[k], r_send.at[k], r_recv.at[k], at(0)).wait_recv()
    covar = (acc[0] + back[0] + back[1]) / (members - 1)
    for j in range(pieces):
        covar_flat[pl.ds(j, levels, stride=pieces), :] = covar[:, j * LANES:(j + 1) * LANES]
    image_dual = covar_flat[...] + search_incr[...] - prior
    out[3] = resid_dual[...] - alpha * image_dual

    for copy in started:
        copy.wait_send()

    def sent(t, carry):
        to_west(t).wait_send()
        to_east(t).wait_send()

        @pl.when(jnp.logical_and(parity == 0, by_relay(t)))
        def _():
            from_relay(t).wait_send()

        return carry

    lax.fori_loop(0, CHUNKS, sent, 0)


def local(wins, bands, lats, *args):
    fields = list(args)
    _, members, levels, _, block = args[9].shape
    flat = levels * block // LANES
    for k in (0, 1, 2, 3, 4, 5, 6, 7, 8, 11, 12):
        fields[k] = args[k].reshape(flat, LANES)
    fields[9] = args[9].reshape(members * levels, block)
    fields[10] = args[10].reshape(5 * flat, LANES)
    fields[14] = args[14][0]
    colors = wins * lats
    share = block // colors
    total = members * levels
    vmem = pl.BlockSpec(memory_space=pltpu.VMEM)
    specs = [pl.BlockSpec(memory_space=pl.ANY)] * 15
    specs[13] = pl.BlockSpec(memory_space=pltpu.SMEM)
    dma = pltpu.SemaphoreType.DMA
    pairs = [(3, CHUNKS), (2,), (2,), (wins,), (wins,), (5,), (bands,), (colors,), (2,), (2,)]
    out = pl.pallas_call(
        functools.partial(kernel, (wins, bands, lats, members, levels, block)),
        out_shape=jax.ShapeDtypeStruct((6, flat, LANES), F32),
        in_specs=specs,
        out_specs=vmem,
        scratch_shapes=[
            pltpu.VMEM(fields[k].shape, fields[k].dtype) for k in range(15) if k != 13
        ] + [
            dma((14,)),
            pltpu.VMEM((2, total, block), BF16),
            pltpu.VMEM((total, block), BF16),
            pltpu.VMEM((2, levels, block), F32),
            pltpu.VMEM((levels, block), F32),
            pltpu.VMEM((3, block, block), BF16),
            pltpu.VMEM((WEIGHTS, share, block), BF16),
            pltpu.VMEM((WEIGHTS, block, block), BF16),
            pltpu.VMEM((7, levels, block), F32),
            pltpu.VMEM((7, levels, block), F32),
            pltpu.VMEM((2, levels, LANES), F32),
            pltpu.VMEM((2, 2, levels, LANES), F32),
            pltpu.VMEM((8, LANES), F32),
            pltpu.VMEM((bands, 8, LANES), F32),
            pltpu.VMEM((8, LANES), F32),
            pltpu.VMEM((colors, 8, LANES), F32),
            pltpu.VMEM((2, flat, LANES), F32),
            pltpu.VMEM((2, flat, LANES), F32),
            pltpu.VMEM((3, levels, block), F32),
            pltpu.VMEM((2, levels, block), F32),
            pltpu.VMEM((flat, LANES), F32),
        ] + [dma(shape) for shape in pairs for _ in range(2)],
        compiler_params=pltpu.CompilerParams(
            collective_id=0, has_side_effects=True, vmem_limit_bytes=60 * 1024 * 1024
        ),
    )(*fields)
    return tuple(out[k].reshape(args[0].shape) for k in range(6))


def solution(mesh):
    wins, bands, lats = (mesh.shape[name] for name in ("win", "lon", "lat"))
    field = P("win", None, "lat", "lon")
    deep = P("win", None, None, "lat", "lon")
    return jax.shard_map(
        functools.partial(local, wins, bands, lats),
        mesh=mesh,
        in_specs=(field,) * 9 + (deep, deep, field, field, P("lon", None), P("lon", None, None, None)),
        out_specs=(field,) * 6,
        check_vma=False,
    )
```

profile of v0, /device:TPU:0, one launch (start us, length us, event | category | flops | bytes accessed | tf_op | source)
XLA Modules:
  0.0 63.0 jit_solution(5649805787463677653)
XLA Ops:
  0.6 60.9 %shard_map.190 = f32[6,64,128]{2,1,0:T(8,128)} custom-call(f32[64,128]{1,0:T(8,128)} %bitcast.23, f32[64,128]{1,0:T(8,128)} %bitcast.24, f32[64,128]{1,0:T(8,128)} %bitcast.25, f32[64,128]{1,0:T(8,128)} %bitcast.26, f32[64,128]{1,0:T(8,128)} %bitcast.27, f32[64,128]{1,0:T(8,128)} %bitcast.28, f32[64,128]{1,0:T(8,128)} %bitcast.29, f32[64,128]{1,0:T(8,128)} %bitcast.30, ...), custom_call_target="tpu_custom_call" | custom-call | tf_op jit(solution)/shard_map/pallas_call | solution.py:407
  61.5 1.5 %fusion = (f32[1,64,128]{2,1,0:T(8,128)}, f32[1,64,128]{2,1,0:T(8,128)}, f32[1,64,128]{2,1,0:T(8,128)}, f32[1,64,128]{2,1,0:T(8,128)}, f32[1,64,128]{2,1,0:T(8,128)}, /*index=5*/f32[1,64,128]{2,1,0:T(8,128)}) fusion(f32[6,64,128]{2,1,0:T(8,128)} %shard_map.190), kind=kLoop, calls=%fused_computation | loop fusion | bytes 393216 | tf_op jit(solution)/shard_map/slice | solution.py:441
where the time goes:
time: 63.2 us; the launch traced here: 63 us
  Pallas kernels  60.9 us (96%)
  local copies, waits for them, and re-layouts  1.52 us (2%)
  between operations  0.65 us (1%)
    pallas_call x1, Pallas kernels, local(): pl.pallas_call(functools.partial(kernel, (wins, bands, lats, members, lev...  60.9 us
    slice x1, local copies, waits for them, and re-layouts, local(): return tuple((out[k].reshape(args[0].shape) for k in range(6)))  1.52 us

commit v1 on v0

--- a/solution.py
+++ b/solution.py
@@ -7,10 +7,10 @@
 from jax.experimental.pallas import tpu as pltpu
 from jax.sharding import PartitionSpec as P
 
-CHUNKS = 8
-EARLY = 2
+CHUNKS = 16
+EARLY = 4
 WEIGHTS = 4
-LAG = 4
+LAG = 6
 LANES = 128
 MESH = pl.DeviceIdType.MESH
 BF16 = jnp.bfloat16
@@ -109,7 +109,7 @@
         return remote(ens.at[lines(t)], near.at[0, lines(t)], e_send.at[1, t], e_recv.at[1, t], at(1))
 
     def by_relay(t):
-        return jnp.logical_or(t < 3, lax.rem(t, 2) == 0)
+        return jnp.logical_or(lax.rem(t, 8) < 3, lax.rem(t, 2) == 0)
 
     def to_relay(t):
         way = -1
@@ -151,7 +151,7 @@
 
     loads[0].wait()
     pl.semaphore_wait(barrier, len(greeted))
-    lax.fori_loop(0, 1, first_sends, 0)
+    lax.fori_loop(0, 2, first_sends, 0)
 
     def slot_of(step):
         target = lax.rem(lon + step + bands, bands)
@@ -185,7 +185,7 @@
         both = pl.ds(2 * k, 2)
         go(remote(w_out.at[both], w_in.at[both, mine], w_send.at[k], w_recv.at[k], at(way)))
 
-    lax.fori_loop(1, 2 * EARLY, first_sends, 0)
+    lax.fori_loop(2, 2 * EARLY, first_sends, 0)
 
     loads[4].wait()
     for c in range(5):

time: 63.2 us -> 67.7 us (1.071)
  Pallas kernels: 60.9 us -> 65.3 us
    pallas_call x1, Pallas kernels: 60.9 us -> 65.3 us  [local(): pl.pallas_call(functools.partial(kernel, (wins, bands, lats, members, lev...]
where the time goes in v1:
time: 67.7 us; the launch traced here: 67.5 us
  Pallas kernels  65.3 us (96%)
  local copies, waits for them, and re-layouts  1.52 us (2%)
    pallas_call x1, Pallas kernels, local(): pl.pallas_call(functools.partial(kernel, (wins, bands, lats, members, lev...  65.3 us
    slice x1, local copies, waits for them, and re-layouts, local(): return tuple((out[k].reshape(args[0].shape) for k in range(6)))  1.52 us

profile of v1, /device:TPU:0, one launch (start us, length us, event | category | flops | bytes accessed | tf_op | source)
XLA Modules:
  0.0 67.5 jit_solution(11340356719574023421)
XLA Ops:
  0.6 65.3 %shard_map.190 = f32[6,64,128]{2,1,0:T(8,128)} custom-call(f32[64,128]{1,0:T(8,128)} %bitcast.23, f32[64,128]{1,0:T(8,128)} %bitcast.24, f32[64,128]{1,0:T(8,128)} %bitcast.25, f32[64,128]{1,0:T(8,128)} %bitcast.26, f32[64,128]{1,0:T(8,128)} %bitcast.27, f32[64,128]{1,0:T(8,128)} %bitcast.28, f32[64,128]{1,0:T(8,128)} %bitcast.29, f32[64,128]{1,0:T(8,128)} %bitcast.30, ...), custom_call_target="tpu_custom_call" | custom-call | tf_op jit(solution)/shard_map/pallas_call | solution.py:407
  66.0 1.5 %fusion = (f32[1,64,128]{2,1,0:T(8,128)}, f32[1,64,128]{2,1,0:T(8,128)}, f32[1,64,128]{2,1,0:T(8,128)}, f32[1,64,128]{2,1,0:T(8,128)}, f32[1,64,128]{2,1,0:T(8,128)}, /*index=5*/f32[1,64,128]{2,1,0:T(8,128)}) fusion(f32[6,64,128]{2,1,0:T(8,128)} %shard_map.190), kind=kLoop, calls=%fused_computation | loop fusion | bytes 393216 | tf_op jit(solution)/shard_map/slice | solution.py:441
